TPU v7x, 32 devices: a whole 2x2x4 slice. The times are simulated.
32 devices in a mesh: group: 2 (over y), expert: 4 (over x, core), dp: 4 (over z).
Axes of the slice: x: 2, y: 2, z: 4, core: 2. Of those that a mesh axis runs over, the one named last changes fastest.
Arguments:
- cotangent: bfloat16 [8192, 7168], P(('group', 'expert', 'dp')), parts along dimension 0, may hold values from -6 to 6
- expert_ids: int32 [8192, 8], P(('group', 'expert', 'dp')), parts along dimension 0, may hold values from 0 to 255, all different within a row; in each aligned block of 128 rows (0 to 127, 128 to 255, ...) at most 8 rows name the same one
- gate_values: float32 [8192, 8], P(('group', 'expert', 'dp')), parts along dimension 0, may hold values from 0.02 to 0.3
- hidden: bfloat16 [8, 4, 4, 2, 8, 1024], P(('group', 'expert'), 'dp'), parts along dimension 0, may hold values from -6 to 6
- down_weight: bfloat16 [4, 1024, 7168], P('expert', None, 'dp'), may hold values from -0.1875 to 0.1875
Outputs:
- fisher: float32 [8, 1024, 7168], P(('group', 'expert'), None, 'dp'), parts along dimension 0
- hidden_grad: bfloat16 [8, 4, 4, 2, 8, 1024], P(('group', 'expert'), 'dp'), parts along dimension 0
There are 2 independent parts, one for each index of `group`. A program takes and returns all parts, laid end to end along the dimension named above; an argument that names none is the same for every part. Nothing has to cross between parts.
Inputs may be any that keep to these rules, and one draw needn't show every extreme that they name: `expert_ids`: each token names 8 different experts. In each aligned block of 128 tokens no expert is named by more than 8 tokens, a bound that some block reaches.
All inputs are finite; a program needn't handle non-finite values.
Results may differ from a plain program's by a relative error of at most 0.0051.
Values may be sent and summed in bfloat16 or wider, within the bound.
A program may use at most 128 MiB of HBM per device.

v0:
```python
import jax
import jax.numpy as jnp
from jax import lax
from jax.sharding import PartitionSpec as P

GROUP = 128


def per_device(cotangent, expert_ids, gate_values, hidden, down_weight):
    experts = lax.axis_size("expert")
    ways = lax.axis_size("dp")
    width = cotangent.shape[1]
    capacity = hidden.shape[4]
    groups_dev = hidden.shape[3]
    hidden_units = hidden.shape[5]
    window = jnp.arange(experts, dtype=jnp.int32)
    match = expert_ids[:, :, None] == window[None, None, :]
    chosen = jnp.any(match, axis=1).astype(jnp.int32).reshape(groups_dev, GROUP, experts)
    weight_sel = jnp.sum(jnp.where(match, gate_values[:, :, None], jnp.float32(0.0)), axis=1)
    weight_sel = weight_sel.reshape(groups_dev, GROUP, experts)
    rank = jnp.cumsum(chosen, axis=1) - 1
    slots = jnp.arange(capacity, dtype=jnp.int32)
    place = (rank[..., None] == slots) & (chosen[..., None] == 1)
    slot_gate = jnp.sum(jnp.where(place, weight_sel[..., None], jnp.float32(0.0)), axis=1)
    token_rows = cotangent.reshape(groups_dev, GROUP, width)
    picked = jnp.einsum(
        "jgec,jgd->ejcd", place.astype(jnp.bfloat16), token_rows, preferred_element_type=jnp.float32
    )
    routed = (picked * jnp.transpose(slot_gate, (1, 0, 2))[..., None]).astype(jnp.bfloat16)
    columns = lax.all_to_all(
        lax.all_to_all(routed[None], "expert", split_axis=1, concat_axis=1, tiled=True),
        "dp",
        split_axis=4,
        concat_axis=0,
        tiled=True,
    )
    flat_cols = columns.reshape(-1, columns.shape[4])
    grad_rows = lax.psum_scatter(
        lax.dot_general(
            flat_cols, down_weight[0], (((1,), (1,)), ((), ())), preferred_element_type=jnp.float32
        ),
        "dp",
        scatter_dimension=0,
        tiled=True,
    )
    hidden_grad = grad_rows.astype(jnp.bfloat16).reshape(hidden.shape)
    shard_width = columns.shape[4]
    empty_fisher = jnp.zeros((hidden_units, shard_width), jnp.float32)
    piece = lax.all_gather(hidden, "dp", axis=1, tiled=True)
    count = piece.shape[1]

    def turn(index, accum):
        source = index // groups_dev
        block = index % groups_dev
        block_h = lax.dynamic_index_in_dim(piece[0], source, 0, keepdims=False)
        block_h = lax.dynamic_index_in_dim(block_h, block, 1, keepdims=False).reshape(
            -1, hidden_units
        )
        block_c = lax.dynamic_index_in_dim(columns, source, 0, keepdims=False)
        block_c = lax.dynamic_index_in_dim(block_c, block, 1, keepdims=False).reshape(
            -1, shard_width
        )
        prod = lax.dot_general(
            block_h, block_c, (((0,), (0,)), ((), ())), preferred_element_type=jnp.float32
        )
        return accum + prod * prod

    fisher_sum = lax.fori_loop(0, count * groups_dev, turn, empty_fisher)
    fisher = (fisher_sum * (1.0 / (ways * groups_dev)))[None]
    return (fisher, hidden_grad)


def solution(mesh):
    in_specs = (
        P(("group", "expert", "dp"), None),
        P(("group", "expert", "dp"), None),
        P(("group", "expert", "dp"), None),
        P(("group", "expert"), "dp", None, None, None, None),
        P("expert", None, "dp"),
    )
    out_specs = (
        P(("group", "expert"), None, "dp"),
        P(("group", "expert"), "dp", None, None, None, None),
    )
    return jax.shard_map(
        per_device, mesh=mesh, in_specs=in_specs, out_specs=out_specs, check_vma=False
    )
```

profile of v0, /device:TPU:0, one launch (start us, length us, event | category | flops | bytes accessed | tf_op | source)
XLA Modules:
  0.0 210.9 jit_solution(8177170741901431970)
XLA Ops:
  7.2 0.7 fusion.10
  7.9 0.1 copy.27
  8.1 0.2 reduce_window_sum.11
  8.3 0.1 copy.28
  8.4 0.7 select_reduce_fusion.1
  9.1 0.1 select_reduce_fusion
  9.2 2.6 %fusion.7 = bf16[1,4,2,8,7168]{4,3,1,2,0:T(8,128)(2,1)S(1)} fusion(bf16[2,128,7168,1]{2,1,3,0:T(8,128)(2,1)} %bitcast.49, f32[4,2,8]{2,0,1:T(4,128)S(1)} %bitcast.55, s32[2,128,4]{1,2,0:T(4,128)S(1)} %copy.28, pred[2,128,4]{1,2,0:T(4,128)(4,1)S(1)} %copy.29), kind=kOutput, calls=%fused_computation.9 | convolution fusion | flops 118374400 | bytes 4592896 | tf_op jit(solution)/shard_map/jgec,jgd->ejcd/dot_general | solution.py:26
  11.8 0.1 copy.30
  11.9 17.1 %all_to_all.23 = bf16[1,4,2,8,7168]{4,3,2,0,1:T(8,128)(2,1)S(1)} all-to-all(bf16[1,4,2,8,7168]{4,3,2,0,1:T(8,128)(2,1)S(1)} %copy.30), channel_id=1, replica_groups=mesh['group'=2,'expert'=4,'dp'=4] {'expert'}, dimensions={1} | all-to-all | bytes 1835008 | tf_op jit(solution)/shard_map/all_to_all | solution.py:31
  29.0 14.6 %copy.31 = bf16[1,4,2,8,7168]{3,1,2,0,4:T(4,128)(2,1)} copy(bf16[1,4,2,8,7168]{4,3,2,0,1:T(8,128)(2,1)S(1)} %all_to_all.23) | data formatting | bytes 1835008 | tf_op jit(solution)/shard_map/all_to_all | solution.py:31
  43.6 0.0 copy-start
  43.6 18.8 %reshape.79 = bf16[4,2,57344]{2,1,0:T(2,128)(2,1)} reshape(bf16[7168,1,2,4,8]{4,3,2,1,0:T(4,128)(2,1)} %bitcast.47) | data formatting | bytes 1835008
  62.4 4.9 %all-to-all-start.1 = ((bf16[4,2,57344]{2,1,0:T(2,128)(2,1)}), bf16[4,2,57344]{2,1,0:T(2,128)(2,1)S(1)}, u32[]{:S(2)}, u32[]{:S(2)}) async-start(bf16[4,2,57344]{2,1,0:T(2,128)(2,1)} %reshape.79), calls=%async_computation.1 | async-start | bytes 1835008 | tf_op jit(solution)/shard_map/all_to_all | solution.py:30
  67.2 0.0 reduce-scatter.2.cloned.1.call-start
  67.2 0.0 copy-done
  67.3 32.4 %all_gather.3 = bf16[1,4,4,2,8,1024]{5,4,3,2,0,1:T(8,128)(2,1)S(1)} all-gather(bf16[1,1,4,2,8,1024]{5,4,3,2,0,1:T(8,128)(2,1)S(1)} %bitcast.53), channel_id=1, replica_groups=mesh['group'=2,'expert'=4,'dp'=4] {'dp'}, dimensions={1}, use_global_device_ids=true | all-gather | bytes 655360 | tf_op jit(solution)/shard_map/all_gather | solution.py:49
  99.7 0.0 all-to-all-done.1
  99.7 19.4 %reshape.80 = bf16[7168,1,2,4,8]{4,3,2,1,0:T(4,128)(2,1)} reshape(bf16[4,2,57344]{2,1,0:T(2,128)(2,1)S(1)} %all-to-all-done.1) | data formatting | bytes 1835008
  119.0 17.1 %copy.32 = bf16[1,4,2,8,4,1792]{5,3,2,1,4,0:T(8,128)(2,1)S(1)} copy(bf16[1,4,2,8,4,1792]{3,1,2,5,4,0:T(4,128)(2,1)} %bitcast.48) | data formatting | bytes 1835008 | tf_op jit(solution)/shard_map/all_to_all | solution.py:30
  136.2 4.2 %fusion.8 = f32[256,1024]{1,0:T(8,128)} fusion(bf16[256,1792]{1,0:T(8,128)(2,1)S(1)} %bitcast.50, bf16[1,1024,1792]{2,1,0:T(8,128)(2,1)} %param.11), kind=kOutput, calls=%fused_computation.11 | convolution fusion | flops 939524096 | bytes 5636096 | tf_op jit(solution)/shard_map/dot_general | solution.py:39
  140.4 0.0 reduce-scatter.2.cloned.1.call-update
  140.4 55.5 %while.17 = (s32[]{:T(128)}, f32[1024,1792]{1,0:T(8,128)}, bf16[1,4,4,2,8,1024]{5,4,3,2,1,0:T(8,128)(2,1)S(1)}, bf16[4,4,2,8,1792]{4,3,2,1,0:T(8,128)(2,1)S(1)},...) while((s32[]{:T(128)}, f32[1024,1792]{1,0:T(8,128)}, ...), condition=%wide.region_5.6_spmd.clone, body=%wide.region_4.5_spmd.clone.sunk | while | flops 122945560 | bytes 14863173 | solution.py:68
  140.4 4.2 %select_add_fusion.2 = f32[1024,1792]{1,0:T(8,128)} fusion(f32[1024,1792]{1,0:T(8,128)} %get-tuple-element.208, pred[]{:T(512)S(6)} %compare.16, bf16[4,4,2,8,1792]{4,3,2,1,0:T(8,128)(2,1)S(1)} %get-tuple-element.220, s32[]{:T(128)S(6)} %select_n.92, s32[]{:T(128)S(6)} %select_n.95, bf16[1,4,4,2,8,1024]{5,4,3,2,1,0:T(8,128)(2,1)S(1)} %get-tuple-element.219), kind=kOutput, calls=%fused_computation.clone.1 | convolution fusion | flops 122945536 | bytes 14862848 | tf_op jit(solution)/shard_map/while/body/eval_jaxpr/dot_general | solution.py:63
  144.6 7.4 %select_add_fusion.2 = f32[1024,1792]{1,0:T(8,128)} fusion(f32[1024,1792]{1,0:T(8,128)} %get-tuple-element.208, pred[]{:T(512)S(6)} %compare.16, bf16[4,4,2,8,1792]{4,3,2,1,0:T(8,128)(2,1)S(1)} %get-tuple-element.220, s32[]{:T(128)S(6)} %select_n.92, s32[]{:T(128)S(6)} %select_n.95, bf16[1,4,4,2,8,1024]{5,4,3,2,1,0:T(8,128)(2,1)S(1)} %get-tuple-element.219), kind=kOutput, calls=%fused_computation.clone.1 | convolution fusion | flops 122945536 | bytes 14862848 | tf_op jit(solution)/shard_map/while/body/eval_jaxpr/dot_general | solution.py:63
  152.1 7.3 %select_add_fusion.2 = f32[1024,1792]{1,0:T(8,128)} fusion(f32[1024,1792]{1,0:T(8,128)} %get-tuple-element.208, pred[]{:T(512)S(6)} %compare.16, bf16[4,4,2,8,1792]{4,3,2,1,0:T(8,128)(2,1)S(1)} %get-tuple-element.220, s32[]{:T(128)S(6)} %select_n.92, s32[]{:T(128)S(6)} %select_n.95, bf16[1,4,4,2,8,1024]{5,4,3,2,1,0:T(8,128)(2,1)S(1)} %get-tuple-element.219), kind=kOutput, calls=%fused_computation.clone.1 | convolution fusion | flops 122945536 | bytes 14862848 | tf_op jit(solution)/shard_map/while/body/eval_jaxpr/dot_general | solution.py:63
  159.4 7.3 %select_add_fusion.2 = f32[1024,1792]{1,0:T(8,128)} fusion(f32[1024,1792]{1,0:T(8,128)} %get-tuple-element.208, pred[]{:T(512)S(6)} %compare.16, bf16[4,4,2,8,1792]{4,3,2,1,0:T(8,128)(2,1)S(1)} %get-tuple-element.220, s32[]{:T(128)S(6)} %select_n.92, s32[]{:T(128)S(6)} %select_n.95, bf16[1,4,4,2,8,1024]{5,4,3,2,1,0:T(8,128)(2,1)S(1)} %get-tuple-element.219), kind=kOutput, calls=%fused_computation.clone.1 | convolution fusion | flops 122945536 | bytes 14862848 | tf_op jit(solution)/shard_map/while/body/eval_jaxpr/dot_general | solution.py:63
  166.7 7.3 %select_add_fusion.2 = f32[1024,1792]{1,0:T(8,128)} fusion(f32[1024,1792]{1,0:T(8,128)} %get-tuple-element.208, pred[]{:T(512)S(6)} %compare.16, bf16[4,4,2,8,1792]{4,3,2,1,0:T(8,128)(2,1)S(1)} %get-tuple-element.220, s32[]{:T(128)S(6)} %select_n.92, s32[]{:T(128)S(6)} %select_n.95, bf16[1,4,4,2,8,1024]{5,4,3,2,1,0:T(8,128)(2,1)S(1)} %get-tuple-element.219), kind=kOutput, calls=%fused_computation.clone.1 | convolution fusion | flops 122945536 | bytes 14862848 | tf_op jit(solution)/shard_map/while/body/eval_jaxpr/dot_general | solution.py:63
  174.0 7.3 %select_add_fusion.2 = f32[1024,1792]{1,0:T(8,128)} fusion(f32[1024,1792]{1,0:T(8,128)} %get-tuple-element.208, pred[]{:T(512)S(6)} %compare.16, bf16[4,4,2,8,1792]{4,3,2,1,0:T(8,128)(2,1)S(1)} %get-tuple-element.220, s32[]{:T(128)S(6)} %select_n.92, s32[]{:T(128)S(6)} %select_n.95, bf16[1,4,4,2,8,1024]{5,4,3,2,1,0:T(8,128)(2,1)S(1)} %get-tuple-element.219), kind=kOutput, calls=%fused_computation.clone.1 | convolution fusion | flops 122945536 | bytes 14862848 | tf_op jit(solution)/shard_map/while/body/eval_jaxpr/dot_general | solution.py:63
  181.3 7.3 %select_add_fusion.2 = f32[1024,1792]{1,0:T(8,128)} fusion(f32[1024,1792]{1,0:T(8,128)} %get-tuple-element.208, pred[]{:T(512)S(6)} %compare.16, bf16[4,4,2,8,1792]{4,3,2,1,0:T(8,128)(2,1)S(1)} %get-tuple-element.220, s32[]{:T(128)S(6)} %select_n.92, s32[]{:T(128)S(6)} %select_n.95, bf16[1,4,4,2,8,1024]{5,4,3,2,1,0:T(8,128)(2,1)S(1)} %get-tuple-element.219), kind=kOutput, calls=%fused_computation.clone.1 | convolution fusion | flops 122945536 | bytes 14862848 | tf_op jit(solution)/shard_map/while/body/eval_jaxpr/dot_general | solution.py:63
  188.6 7.3 %select_add_fusion.2 = f32[1024,1792]{1,0:T(8,128)} fusion(f32[1024,1792]{1,0:T(8,128)} %get-tuple-element.208, pred[]{:T(512)S(6)} %compare.16, bf16[4,4,2,8,1792]{4,3,2,1,0:T(8,128)(2,1)S(1)} %get-tuple-element.220, s32[]{:T(128)S(6)} %select_n.92, s32[]{:T(128)S(6)} %select_n.95, bf16[1,4,4,2,8,1024]{5,4,3,2,1,0:T(8,128)(2,1)S(1)} %get-tuple-element.219), kind=kOutput, calls=%fused_computation.clone.1 | convolution fusion | flops 122945536 | bytes 14862848 | tf_op jit(solution)/shard_map/while/body/eval_jaxpr/dot_general | solution.py:63
  195.9 6.6 %multiply_bitcast_fusion = f32[1,1024,1792]{2,1,0:T(8,128)} fusion(f32[1024,1792]{1,0:T(8,128)} %get-tuple-element.140), kind=kLoop, calls=%fused_computation.10 | loop fusion | flops 1835008 | bytes 14680064 | tf_op jit(solution)/shard_map/broadcast_in_dim | solution.py:69
  202.5 0.0 reduce-scatter.2.cloned.1.call-done
  202.5 1.6 convert_element_type.26
  (6 shorter events, 0.0 us)
Async XLA Ops:
  43.6 23.7 %copy-start = (bf16[1,1,4,2,8,1024]{5,4,3,2,1,0:T(8,128)(2,1)S(1)}, bf16[1,1,4,2,8,1024]{5,4,3,2,1,0:T(8,128)(2,1)}, u32[]{:S(2)}) copy-start(bf16[1,1,4,2,8,1024]{5,4,3,2,1,0:T(8,128)(2,1)} %param.10) | copy-start | bytes 393220
  62.4 37.3 %all-to-all-start.1 = ((bf16[4,2,57344]{2,1,0:T(2,128)(2,1)}), bf16[4,2,57344]{2,1,0:T(2,128)(2,1)S(1)}, u32[]{:S(2)}, u32[]{:S(2)}) async-start(bf16[4,2,57344]{2,1,0:T(2,128)(2,1)} %reshape.79), calls=%async_computation.1 | async-start | bytes 1835008 | tf_op jit(solution)/shard_map/all_to_all | solution.py:30
  67.2 135.2 %reduce-scatter.2.cloned.1.call-start = ((), (), s32[]{:S(2)}) async-start(), calls=%async_computation.3 | async-start | bytes 1310720 | tf_op jit(solution)/shard_map/reduce_scatter | solution.py:38
Sparse Core Ops, SparseCore 0:
  140.5 27.8 reduce-scatter.1
where the time goes:
time: 212 us; the launch traced here: 211 us
  local copies, waits for them, and re-layouts  70.2 us (33%)
  matrix products  62.3 us (29%)
  blocking collectives  49.5 us (23%)
  between operations  14.1 us (7%)
  other arithmetic  10 us (5%)
  starting transfers between devices  4.87 us (2%)
    dot_general x8, matrix products, turn(): lax.dot_general(block_h, block_c, (((0,), (0,)), ((), ())), preferred_ele...  55.4 us
    unnamed x4, local copies, waits for them, and re-layouts  38.2 us
    all_gather x1, blocking collectives, per_device(): piece = lax.all_gather(hidden, 'dp', axis=1, tiled=True)  32.4 us
    all_to_all x1, local copies, waits for them, and re-layouts, per_device(): lax.all_to_all(lax.all_to_all(routed[None], 'expert', split_axis=1, conca...  17.1 us
    all_to_all x1, blocking collectives, per_device(): lax.all_to_all(routed[None], 'expert', split_axis=1, concat_axis=1, tiled...  17.1 us
    all_to_all x1, local copies, waits for them, and re-layouts, per_device(): lax.all_to_all(routed[None], 'expert', split_axis=1, concat_axis=1, tiled...  14.6 us
    broadcast_in_dim x1, other arithmetic, per_device(): fisher = (fisher_sum * (1.0 / (ways * groups_dev)))[None]  6.6 us
    all_to_all x1, starting transfers between devices, per_device(): lax.all_to_all(lax.all_to_all(routed[None], 'expert', split_axis=1, conca...  4.87 us
  transfers between devices with their start and end apart: 2, of which 0 were waited for; matrix products, arithmetic and copies ran while one was open for 29% of the time, Pallas kernels for 0%

commit v1 on v0

--- a/solution.py
+++ b/solution.py
@@ -2,8 +2,25 @@
 import jax.numpy as jnp
 from jax import lax
 from jax.sharding import PartitionSpec as P
+from jax.lax import axis_index, axis_size, ppermute
 
 GROUP = 128
+
+
+def _note_threads(s0, axis_k, xin):
+    current_block = s0.shape
+    r_now = s0.reshape(
+        *current_block[:axis_k], xin, current_block[axis_k] // xin, *current_block[axis_k + 1 :]
+    )
+    low = jnp.moveaxis(r_now, axis_k, 0)
+    return low
+
+
+def run_shelves_here(block_here, in_dim):
+    row_out = list(block_here.shape[1:])
+    row_out[in_dim] *= block_here.shape[0]
+    e_next = jnp.moveaxis(block_here, 0, in_dim).reshape(row_out)
+    return e_next
 
 
 def per_device(cotangent, expert_ids, gate_values, hidden, down_weight):
@@ -27,12 +44,26 @@
         "jgec,jgd->ejcd", place.astype(jnp.bfloat16), token_rows, preferred_element_type=jnp.float32
     )
     routed = (picked * jnp.transpose(slot_gate, (1, 0, 2))[..., None]).astype(jnp.bfloat16)
+
+    def push_knots_here(along_axis, q_in, mine_x, base_x):
+        part_now = axis_index(along_axis)
+        y = axis_size(along_axis)
+        met_up, new = (y, part_now)
+        everything = _note_threads(base_x, q_in, met_up)
+        row_list = [everything[new]]
+        for pp in range(1, met_up):
+            a_next = everything[(new + pp) % met_up]
+            then = ppermute(
+                a_next, along_axis, [(dev_j, (dev_j + pp) % met_up) for dev_j in range(met_up)]
+            )
+            row_list.append(then)
+        reached = jnp.stack(row_list)
+        everything = reached[(new - jnp.arange(met_up)) % met_up]
+        last = run_shelves_here(everything, mine_x)
+        return last
+
     columns = lax.all_to_all(
-        lax.all_to_all(routed[None], "expert", split_axis=1, concat_axis=1, tiled=True),
-        "dp",
-        split_axis=4,
-        concat_axis=0,
-        tiled=True,
+        push_knots_here("expert", 1, 1, routed[None]), "dp", split_axis=4, concat_axis=0, tiled=True
     )
     flat_cols = columns.reshape(-1, columns.shape[4])
     grad_rows = lax.psum_scatter(

time: 212 us -> 236 us (1.11)
  local copies, waits for them, and re-layouts: 70.2 us -> 96.3 us
  blocking collectives: 49.5 us -> 33.9 us
  waiting for transfers between devices: 0.02 us -> 8.87 us
  starting transfers between devices: 4.87 us -> 9.33 us
    another operation x0 -> x1, local copies, waits for them, and re-layouts: none -> 24.1 us  [run_shelves_here(): e_next = jnp.moveaxis(block_here, 0, in_dim).reshape(row_out)]
    all_to_all x1 -> x0, blocking collectives: 17.1 us -> none  [per_device(): lax.all_to_all(routed[None], 'expert', split_axis=1, concat_axis=1, tiled...]
    ppermute x0 -> x3, waiting for transfers between devices: none -> 8.84 us  [push_knots_here(): ppermute(a_next, along_axis, [(dev_j, (dev_j + pp) % met_up) for dev_j in...]
    ppermute x0 -> x3, starting transfers between devices: none -> 4.46 us  [push_knots_here(): ppermute(a_next, along_axis, [(dev_j, (dev_j + pp) % met_up) for dev_j in...]
    unnamed x4 -> x5, local copies, waits for them, and re-layouts: 38.2 us -> 38.3 us
  transfers between devices with their start and end apart: 2 -> 5, of which waited for: 0 -> 3; matrix products, arithmetic and copies ran while one was open for 29% -> 26% of each run, Pallas kernels for 0% -> 0%
where the time goes in v1:
time: 236 us; the launch traced here: 235 us
  local copies, waits for them, and re-layouts  96.3 us (41%)
  matrix products  62.3 us (26%)
  blocking collectives  33.9 us (14%)
  between operations  14.2 us (6%)
  other arithmetic  10.1 us (4%)
  starting transfers between devices  9.33 us (4%)
  waiting for transfers between devices  8.87 us (4%)
    dot_general x8, matrix products, turn(): lax.dot_general(block_h, block_c, (((0,), (0,)), ((), ())), preferred_ele...  55.4 us
    unnamed x5, local copies, waits for them, and re-layouts  38.3 us
    all_gather x1, blocking collectives, per_device(): piece = lax.all_gather(hidden, 'dp', axis=1, tiled=True)  33.9 us
    all_to_all x2, local copies, waits for them, and re-layouts, per_device(): lax.all_to_all(push_knots_here('expert', 1, 1, routed[None]), 'dp', split...  33 us
    another operation x1, local copies, waits for them, and re-layouts, run_shelves_here(): e_next = jnp.moveaxis(block_here, 0, in_dim).reshape(row_out)  24.1 us
    ppermute x3, waiting for transfers between devices, push_knots_here(): ppermute(a_next, along_axis, [(dev_j, (dev_j + pp) % met_up) for dev_j in...  8.84 us
    broadcast_in_dim x1, other arithmetic, per_device(): fisher = (fisher_sum * (1.0 / (ways * groups_dev)))[None]  6.6 us
    all_to_all x1, starting transfers between devices, per_device(): lax.all_to_all(push_knots_here('expert', 1, 1, routed[None]), 'dp', split...  4.87 us
  transfers between devices with their start and end apart: 5, of which 3 were waited for; matrix products, arithmetic and copies ran while one was open for 26% of the time, Pallas kernels for 0%

profile of v1, /device:TPU:0, one launch (start us, length us, event | category | flops | bytes accessed | tf_op | source)
XLA Modules:
  0.0 235.0 jit_solution(10493241282755671862)
XLA Ops:
  7.2 0.7 fusion.9
  7.9 0.1 copy.42
  8.1 0.2 reduce_window_sum.11
  8.3 0.1 copy.43
  8.4 0.7 select_reduce_fusion.1
  9.2 0.1 select_reduce_fusion
  9.3 2.6 %fusion.6 = bf16[4,2,8,7168]{3,2,0,1:T(8,128)(2,1)S(1)} fusion(bf16[2,128,7168,1]{2,1,3,0:T(8,128)(2,1)} %bitcast.62, f32[4,2,8]{2,0,1:T(4,128)S(1)} %bitcast.71, s32[2,128,4]{1,2,0:T(4,128)S(1)} %copy.43, pred[2,128,4]{1,2,0:T(4,128)(4,1)S(1)} %copy.44), kind=kOutput, calls=%fused_computation.9 | convolution fusion | flops 118374400 | bytes 4592896 | tf_op jit(solution)/shard_map/jgec,jgd->ejcd/dot_general | solution.py:43
  11.9 0.1 dynamic-slice_bitcast_fusion.3
  12.0 0.5 collective-permute-start
  12.5 2.6 %collective-permute-start.1 = (bf16[1,1,2,8,7168]{4,3,2,1,0:T(8,128)(2,1)S(1)}, bf16[1,1,2,8,7168]{4,3,2,1,0:T(8,128)(2,1)S(1)}, u32[]{:S(2)}, u32[]{:S(2)}) collective-permute-start(bf16[1,1,2,8,7168]{4,3,2,1,0:T(8,128)(2,1)S(1)} %get-tuple-element.186), channel_id=1, source_target_pairs={{0,8},{4,12},{8,0},{12,4},{1,9},{5,13},{9,1},{13,5},{2,10},{6,14},... | collective-permute-start | bytes 688136 | tf_op jit(solution)/shard_map/ppermute | solution.py:56
  15.1 1.4 collective-permute-start.2
  16.5 3.2 %collective-permute-done = bf16[1,1,2,8,7168]{4,3,2,1,0:T(8,128)(2,1)S(1)} collective-permute-done((bf16[1,1,2,8,7168]{4,3,2,1,0:T(8,128)(2,1)S(1)}, bf16[1,1,2,8,7168]{4,3,2,1,0:T(8,128)(2,1)S(1)}, u32[]{:S(2)}, u32[]{:S(2)}) %collective-permute-start) | collective-permute-done | bytes 229408 | tf_op jit(solution)/shard_map/ppermute | solution.py:56
  19.7 1.8 collective-permute-done.1
  21.5 3.8 %collective-permute-done.2 = bf16[1,1,2,8,7168]{4,3,2,1,0:T(8,128)(2,1)S(1)} collective-permute-done((bf16[1,1,2,8,7168]{4,3,2,1,0:T(8,128)(2,1)S(1)}, bf16[1,1,2,8,7168]{4,3,2,1,0:T(8,128)(2,1)S(1)}, u32[]{:S(2)}, u32[]{:S(2)}) %collective-permute-start.2) | collective-permute-done | bytes 229408 | tf_op jit(solution)/shard_map/ppermute | solution.py:56
  25.3 0.1 maximum_bitcast_fusion
  25.4 0.6 gather_fusion
  26.1 24.1 %copy.45 = bf16[1,4,2,8,7168]{3,2,1,0,4:T(2,128)(2,1)} copy(bf16[1,4,2,8,7168]{4,3,2,1,0:T(8,128)(2,1)S(1)} %bitcast.63) | data formatting | bytes 1835008 | tf_op jit(solution)/shard_map/reshape;transpose | solution.py:22
  50.1 0.0 copy-start
  50.1 18.8 %reshape.150 = bf16[4,2,57344]{2,1,0:T(2,128)(2,1)} reshape(bf16[7168,1,4,2,8]{4,3,2,1,0:T(2,128)(2,1)} %bitcast.58) | data formatting | bytes 1835008
  68.9 4.9 %all-to-all-start = ((bf16[4,2,57344]{2,1,0:T(2,128)(2,1)}), bf16[4,2,57344]{2,1,0:T(2,128)(2,1)S(1)}, u32[]{:S(2)}, u32[]{:S(2)}) async-start(bf16[4,2,57344]{2,1,0:T(2,128)(2,1)} %reshape.150), calls=%async_computation | async-start | bytes 1835008 | tf_op jit(solution)/shard_map/all_to_all | solution.py:65
  73.8 0.0 reduce-scatter.2.cloned.1.call-start
  73.8 0.0 copy-done
  73.8 33.9 %all_gather.3 = bf16[1,4,4,2,8,1024]{5,4,3,2,0,1:T(8,128)(2,1)S(1)} all-gather(bf16[1,1,4,2,8,1024]{5,4,3,2,0,1:T(8,128)(2,1)S(1)} %bitcast.69), channel_id=1, replica_groups=mesh['group'=2,'expert'=4,'dp'=4] {'dp'}, dimensions={1}, use_global_device_ids=true | all-gather | bytes 655360 | tf_op jit(solution)/shard_map/all_gather | solution.py:80
  107.7 0.0 all-to-all-done
  107.7 19.4 %reshape.151 = bf16[7168,1,4,2,8]{4,3,2,1,0:T(2,128)(2,1)} reshape(bf16[4,2,57344]{2,1,0:T(2,128)(2,1)S(1)} %all-to-all-done) | data formatting | bytes 1835008
  127.1 32.9 %copy.51 = bf16[1,4,2,8,4,1792]{5,4,3,2,1,0:T(4,128)(2,1)S(1)} copy(bf16[1,4,2,8,4,1792]{3,2,1,5,4,0:T(2,128)(2,1)} %bitcast.59) | data formatting | bytes 1835008 | tf_op jit(solution)/shard_map/all_to_all | solution.py:65
  160.0 0.1 copy.48
  160.1 0.1 copy.49
  160.2 4.2 %fusion.7 = f32[256,1024]{1,0:T(8,128)} fusion(bf16[256,1792]{1,0:T(8,128)(2,1)S(1)} %bitcast.65, bf16[1,1024,1792]{2,1,0:T(8,128)(2,1)} %param.11), kind=kOutput, calls=%fused_computation.11 | convolution fusion | flops 939524096 | bytes 5636096 | tf_op jit(solution)/shard_map/dot_general | solution.py:70
  164.4 0.0 reduce-scatter.2.cloned.1.call-update
  164.4 55.5 %while.17 = (s32[]{:T(128)}, f32[1024,1792]{1,0:T(8,128)}, bf16[1,4,4,2,8,1024]{5,4,3,2,1,0:T(8,128)(2,1)S(1)}, bf16[4,4,2,8,1792]{4,3,2,1,0:T(8,128)(2,1)S(1)},...) while((s32[]{:T(128)}, f32[1024,1792]{1,0:T(8,128)}, ...), condition=%wide.region_5.6_spmd.clone, body=%wide.region_4.5_spmd.clone.sunk | while | flops 122945560 | bytes 14863173 | solution.py:99
  164.4 4.2 %select_add_fusion.2 = f32[1024,1792]{1,0:T(8,128)} fusion(f32[1024,1792]{1,0:T(8,128)} %get-tuple-element.224, pred[]{:T(512)S(6)} %compare.26, bf16[4,4,2,8,1792]{4,3,2,1,0:T(8,128)(2,1)S(1)} %get-tuple-element.236, s32[]{:T(128)S(6)} %select_n.159, s32[]{:T(128)S(6)} %select_n.162, bf16[1,4,4,2,8,1024]{5,4,3,2,1,0:T(8,128)(2,1)S(1)} %get-tuple-element.235), kind=kOutput, calls=%fused_computation.1.clone.1 | convolution fusion | flops 122945536 | bytes 14862848 | tf_op jit(solution)/shard_map/while/body/eval_jaxpr/dot_general | solution.py:94
  168.6 7.5 %select_add_fusion.2 = f32[1024,1792]{1,0:T(8,128)} fusion(f32[1024,1792]{1,0:T(8,128)} %get-tuple-element.224, pred[]{:T(512)S(6)} %compare.26, bf16[4,4,2,8,1792]{4,3,2,1,0:T(8,128)(2,1)S(1)} %get-tuple-element.236, s32[]{:T(128)S(6)} %select_n.159, s32[]{:T(128)S(6)} %select_n.162, bf16[1,4,4,2,8,1024]{5,4,3,2,1,0:T(8,128)(2,1)S(1)} %get-tuple-element.235), kind=kOutput, calls=%fused_computation.1.clone.1 | convolution fusion | flops 122945536 | bytes 14862848 | tf_op jit(solution)/shard_map/while/body/eval_jaxpr/dot_general | solution.py:94
  176.1 7.3 %select_add_fusion.2 = f32[1024,1792]{1,0:T(8,128)} fusion(f32[1024,1792]{1,0:T(8,128)} %get-tuple-element.224, pred[]{:T(512)S(6)} %compare.26, bf16[4,4,2,8,1792]{4,3,2,1,0:T(8,128)(2,1)S(1)} %get-tuple-element.236, s32[]{:T(128)S(6)} %select_n.159, s32[]{:T(128)S(6)} %select_n.162, bf16[1,4,4,2,8,1024]{5,4,3,2,1,0:T(8,128)(2,1)S(1)} %get-tuple-element.235), kind=kOutput, calls=%fused_computation.1.clone.1 | convolution fusion | flops 122945536 | bytes 14862848 | tf_op jit(solution)/shard_map/while/body/eval_jaxpr/dot_general | solution.py:94
  183.4 7.3 %select_add_fusion.2 = f32[1024,1792]{1,0:T(8,128)} fusion(f32[1024,1792]{1,0:T(8,128)} %get-tuple-element.224, pred[]{:T(512)S(6)} %compare.26, bf16[4,4,2,8,1792]{4,3,2,1,0:T(8,128)(2,1)S(1)} %get-tuple-element.236, s32[]{:T(128)S(6)} %select_n.159, s32[]{:T(128)S(6)} %select_n.162, bf16[1,4,4,2,8,1024]{5,4,3,2,1,0:T(8,128)(2,1)S(1)} %get-tuple-element.235), kind=kOutput, calls=%fused_computation.1.clone.1 | convolution fusion | flops 122945536 | bytes 14862848 | tf_op jit(solution)/shard_map/while/body/eval_jaxpr/dot_general | solution.py:94
  190.7 7.3 %select_add_fusion.2 = f32[1024,1792]{1,0:T(8,128)} fusion(f32[1024,1792]{1,0:T(8,128)} %get-tuple-element.224, pred[]{:T(512)S(6)} %compare.26, bf16[4,4,2,8,1792]{4,3,2,1,0:T(8,128)(2,1)S(1)} %get-tuple-element.236, s32[]{:T(128)S(6)} %select_n.159, s32[]{:T(128)S(6)} %select_n.162, bf16[1,4,4,2,8,1024]{5,4,3,2,1,0:T(8,128)(2,1)S(1)} %get-tuple-element.235), kind=kOutput, calls=%fused_computation.1.clone.1 | convolution fusion | flops 122945536 | bytes 14862848 | tf_op jit(solution)/shard_map/while/body/eval_jaxpr/dot_general | solution.py:94
  198.1 7.3 %select_add_fusion.2 = f32[1024,1792]{1,0:T(8,128)} fusion(f32[1024,1792]{1,0:T(8,128)} %get-tuple-element.224, pred[]{:T(512)S(6)} %compare.26, bf16[4,4,2,8,1792]{4,3,2,1,0:T(8,128)(2,1)S(1)} %get-tuple-element.236, s32[]{:T(128)S(6)} %select_n.159, s32[]{:T(128)S(6)} %select_n.162, bf16[1,4,4,2,8,1024]{5,4,3,2,1,0:T(8,128)(2,1)S(1)} %get-tuple-element.235), kind=kOutput, calls=%fused_computation.1.clone.1 | convolution fusion | flops 122945536 | bytes 14862848 | tf_op jit(solution)/shard_map/while/body/eval_jaxpr/dot_general | solution.py:94
  205.3 7.3 %select_add_fusion.2 = f32[1024,1792]{1,0:T(8,128)} fusion(f32[1024,1792]{1,0:T(8,128)} %get-tuple-element.224, pred[]{:T(512)S(6)} %compare.26, bf16[4,4,2,8,1792]{4,3,2,1,0:T(8,128)(2,1)S(1)} %get-tuple-element.236, s32[]{:T(128)S(6)} %select_n.159, s32[]{:T(128)S(6)} %select_n.162, bf16[1,4,4,2,8,1024]{5,4,3,2,1,0:T(8,128)(2,1)S(1)} %get-tuple-element.235), kind=kOutput, calls=%fused_computation.1.clone.1 | convolution fusion | flops 122945536 | bytes 14862848 | tf_op jit(solution)/shard_map/while/body/eval_jaxpr/dot_general | solution.py:94
  212.6 7.3 %select_add_fusion.2 = f32[1024,1792]{1,0:T(8,128)} fusion(f32[1024,1792]{1,0:T(8,128)} %get-tuple-element.224, pred[]{:T(512)S(6)} %compare.26, bf16[4,4,2,8,1792]{4,3,2,1,0:T(8,128)(2,1)S(1)} %get-tuple-element.236, s32[]{:T(128)S(6)} %select_n.159, s32[]{:T(128)S(6)} %select_n.162, bf16[1,4,4,2,8,1024]{5,4,3,2,1,0:T(8,128)(2,1)S(1)} %get-tuple-element.235), kind=kOutput, calls=%fused_computation.1.clone.1 | convolution fusion | flops 122945536 | bytes 14862848 | tf_op jit(solution)/shard_map/while/body/eval_jaxpr/dot_general | solution.py:94
  219.9 6.6 %multiply_bitcast_fusion = f32[1,1024,1792]{2,1,0:T(8,128)} fusion(f32[1024,1792]{1,0:T(8,128)} %get-tuple-element.140), kind=kLoop, calls=%fused_computation.10 | loop fusion | flops 1835008 | bytes 14680064 | tf_op jit(solution)/shard_map/broadcast_in_dim | solution.py:100
  226.5 0.0 reduce-scatter.2.cloned.1.call-done
  226.5 1.6 convert_element_type.26
  (8 shorter events, 0.1 us)
Async XLA Ops:
  12.0 7.7 %collective-permute-start = (bf16[1,1,2,8,7168]{4,3,2,1,0:T(8,128)(2,1)S(1)}, bf16[1,1,2,8,7168]{4,3,2,1,0:T(8,128)(2,1)S(1)}, u32[]{:S(2)}, u32[]{:S(2)}) collective-permute-start(bf16[1,1,2,8,7168]{4,3,2,1,0:T(8,128)(2,1)S(1)} %get-tuple-element.187), channel_id=1, source_target_pairs={{0,4},{4,8},{8,12},{12,0},{1,5},{5,9},{9,13},{13,1},{2,6},{6,10},{... | collective-permute-start | bytes 688136 | tf_op jit(solution)/shard_map/ppermute | solution.py:56
  12.5 9.0 %collective-permute-start.1 = (bf16[1,1,2,8,7168]{4,3,2,1,0:T(8,128)(2,1)S(1)}, bf16[1,1,2,8,7168]{4,3,2,1,0:T(8,128)(2,1)S(1)}, u32[]{:S(2)}, u32[]{:S(2)}) collective-permute-start(bf16[1,1,2,8,7168]{4,3,2,1,0:T(8,128)(2,1)S(1)} %get-tuple-element.186), channel_id=1, source_target_pairs={{0,8},{4,12},{8,0},{12,4},{1,9},{5,13},{9,1},{13,5},{2,10},{6,14},... | collective-permute-start | bytes 688136 | tf_op jit(solution)/shard_map/ppermute | solution.py:56
  15.1 10.3 %collective-permute-start.2 = (bf16[1,1,2,8,7168]{4,3,2,1,0:T(8,128)(2,1)S(1)}, bf16[1,1,2,8,7168]{4,3,2,1,0:T(8,128)(2,1)S(1)}, u32[]{:S(2)}, u32[]{:S(2)}) collective-permute-start(bf16[1,1,2,8,7168]{4,3,2,1,0:T(8,128)(2,1)S(1)} %get-tuple-element.185), channel_id=1, source_target_pairs={{0,12},{4,0},{8,4},{12,8},{1,13},{5,1},{9,5},{13,9},{2,14},{6,2},{... | collective-permute-start | bytes 688136 | tf_op jit(solution)/shard_map/ppermute | solution.py:56
  50.1 23.7 %copy-start = (bf16[1,1,4,2,8,1024]{5,4,3,2,1,0:T(8,128)(2,1)S(1)}, bf16[1,1,4,2,8,1024]{5,4,3,2,1,0:T(8,128)(2,1)}, u32[]{:S(2)}) copy-start(bf16[1,1,4,2,8,1024]{5,4,3,2,1,0:T(8,128)(2,1)} %param.10) | copy-start | bytes 393220
  68.9 38.8 %all-to-all-start = ((bf16[4,2,57344]{2,1,0:T(2,128)(2,1)}), bf16[4,2,57344]{2,1,0:T(2,128)(2,1)S(1)}, u32[]{:S(2)}, u32[]{:S(2)}) async-start(bf16[4,2,57344]{2,1,0:T(2,128)(2,1)} %reshape.150), calls=%async_computation | async-start | bytes 1835008 | tf_op jit(solution)/shard_map/all_to_all | solution.py:65
  73.8 152.7 %reduce-scatter.2.cloned.1.call-start = ((), (), s32[]{:S(2)}) async-start(), calls=%async_computation.2 | async-start | bytes 1310720 | tf_op jit(solution)/shard_map/reduce_scatter | solution.py:69
Sparse Core Ops, SparseCore 0:
  164.5 27.2 reduce-scatter.1
